TPU v7x, 512 devices: a whole 4x8x8 slice. The times are simulated.
512 devices in a mesh: slab: 128 (over y, z, core), grp: 4 (over x).
Axes of the slice: x: 4, y: 8, z: 8, core: 2. Of those that a mesh axis runs over, the one named last changes fastest.
Arguments:
- u_now: float32 [3, 2048, 32, 128], P(None, 'slab', 'grp'), may hold values from -6 to 6
- u_prev: float32 [3, 2048, 32, 128], P(None, 'slab', 'grp'), may hold values from -6 to 6
- force: float32 [3, 2048, 32, 128], P(None, 'slab', 'grp'), may hold values from -6 to 6
- stiffness: float32 [2048, 32, 128], P('slab', 'grp'), may hold values from 0.5 to 2
- broken: int32 [512, 8, 32], P('slab', 'grp'), may hold values 0 or 1
- flags: int32 [512, 8, 32], P('slab', 'grp'), may hold values 0 or 1
Outputs:
- displacement: float32 [3, 2048, 32, 128], P(None, 'slab', 'grp')
- coeffs: float32 [6, 32, 128, 2048], P(None, 'grp', 'slab')
All inputs are finite; a program needn't handle non-finite values. No bound on the sum of `broken` or of `flags` on one device may be relied on, other than what follows from the above.
Results may differ from a plain program's by a relative error of at most 0.0001.
Values sent between devices are 32-bit elements; how exact they have to be, the bound alone decides.
No kernel may reach another device: no remote copies, remote signals or barrier semaphores. Data moves between devices by JAX's collectives and lax.ppermute only.
A program may use at most 64 MiB of HBM per device.

v0:
```python
import jax
import jax.numpy as jnp
import numpy as np
from jax import lax
from jax.sharding import PartitionSpec as P

STEPS = 2
ITERS = 2
LEVELS = 3
SPRING_NORMAL = 1.0
SPRING_SHEAR = 0.4
MASS_TERM = 1.0
CRACK_CUT = 0.9


def with_halo(block, sides, width):
    for axis, dim in sides:
        count = lax.axis_size(axis)
        forward = [(i, i + 1) for i in range(count - 1)]
        backward = [(target, source) for source, target in forward]
        low = lax.ppermute(
            lax.slice_in_dim(block, block.shape[dim] - width, None, axis=dim), axis, forward
        )
        high = lax.ppermute(lax.slice_in_dim(block, 0, width, axis=dim), axis, backward)
        block = jnp.concatenate([low, block, high], axis=dim)
    return block


def cosine_table():
    freq = np.arange(4)[:, None]
    place = np.arange(4)[None, :]
    factor = np.where(freq == 0, 0.5, np.sqrt(0.5))
    return factor * np.cos(np.pi * (2 * place + 1) * freq / 8.0)


def block_table(count):
    return jnp.asarray(np.kron(np.eye(count // 4), cosine_table()), jnp.float32)


def spread(mask):
    values = mask.astype(jnp.float32)
    size_a, size_b, size_c = values.shape
    wide = jnp.broadcast_to(values[:, None, :, None, :, None], (size_a, 4, size_b, 4, size_c, 4))
    return wide.reshape(size_a * 4, size_b * 4, size_c * 4)


def sides(padded, axis_index):
    leading = padded.ndim - 3

    def cut(offset):
        index_list = [slice(None)] * leading + [slice(1, -1)] * 3
        length = padded.shape[leading + axis_index]
        index_list[leading + axis_index] = slice(1 + offset, length - 1 + offset)
        return padded[tuple(index_list)]

    return (cut(1), cut(-1))


def springs(field, weight, field_pad, weight_pad):
    result = MASS_TERM * field
    for axis_index in range(3):
        upper_v, lower_v = sides(field_pad, axis_index)
        upper_w, lower_w = sides(weight_pad, axis_index)
        k_upper = 0.5 * (weight + upper_w)
        k_lower = 0.5 * (weight + lower_w)
        change = k_upper * (field - upper_v) + k_lower * (field - lower_v)
        coupling = jnp.array(
            [SPRING_NORMAL if comp == axis_index else SPRING_SHEAR for comp in range(3)],
            jnp.float32,
        ).reshape(3, 1, 1, 1)
        result = result + coupling * change
    return result


def faces(field):
    padded = with_halo(field, (("slab", 1), ("grp", 2)), 1)
    return jnp.pad(padded, ((0, 0), (0, 0), (0, 0), (1, 1)))


def stresses(carry, field_pad):
    rows_out = []
    for axis_index in range(3):
        upper_v, lower_v = sides(field_pad, axis_index)
        rows_out.append(SPRING_NORMAL * carry * 0.5 * (upper_v[axis_index] - lower_v[axis_index]))
    return jnp.stack(rows_out)


def single_sum(value):
    return lax.psum(value, ("slab", "grp"))


def lift(signal):
    even = signal[..., 0::2]
    odd = signal[..., 1::2]
    detail = odd - 0.5 * (even + jnp.roll(even, -1, axis=-1))
    approx = even + 0.25 * (jnp.roll(detail, 1, axis=-1) + detail)
    return (approx, detail)


def wavelet(signal):
    pieces = []
    approx = signal
    for level_index in range(LEVELS):
        approx, detail = lift(approx)
        pieces.insert(0, detail)
    return jnp.concatenate([approx] + pieces, axis=-1)


def body(u_now, u_prev, force, stiffness, broken, flags):
    weight = stiffness * (1.0 - CRACK_CUT * spread(broken))
    carry = spread(flags) * weight
    weight_pad = with_halo(weight, (("slab", 0), ("grp", 1)), 1)
    weight_pad = jnp.pad(weight_pad, ((0, 0), (0, 0), (1, 1)))

    def operate(field):
        return springs(field, weight, faces(field), weight_pad)

    for step_index in range(STEPS):
        rhs = MASS_TERM * (2.0 * u_now - u_prev) + force
        guess = u_now
        residual = rhs - operate(guess)
        direction = residual
        norm_now = single_sum(jnp.sum(residual * residual))
        for turn_index in range(ITERS):
            image = operate(direction)
            alpha = norm_now / single_sum(jnp.sum(direction * image))
            guess = guess + alpha * direction
            residual = residual - alpha * image
            if turn_index + 1 < ITERS:
                norm_next = single_sum(jnp.sum(residual * residual))
                direction = residual + norm_next / norm_now * direction
                norm_now = norm_next
        u_prev = u_now
        u_now = guess
    stress = stresses(carry, faces(u_now))
    fields = jnp.concatenate([u_now, stress], axis=0)
    table_x = block_table(fields.shape[1])
    table_y = block_table(fields.shape[2])
    table_z = block_table(fields.shape[3])
    blockc = jnp.einsum("ax,hxyz->hayz", table_x, fields, precision=lax.Precision.HIGHEST)
    blockc = jnp.einsum("by,hxyz->hxbz", table_y, blockc, precision=lax.Precision.HIGHEST)
    blockc = jnp.einsum("hxyz,cz->hxyc", blockc, table_z, precision=lax.Precision.HIGHEST)
    moved = jnp.transpose(blockc, (0, 2, 3, 1))
    shipped = lax.all_to_all(moved, "slab", split_axis=2, concat_axis=3, tiled=True)
    coeffs = wavelet(shipped)
    return (u_now, coeffs)


def solution(mesh):
    return jax.shard_map(
        body,
        mesh=mesh,
        in_specs=(
            P(None, "slab", "grp", None),
            P(None, "slab", "grp", None),
            P(None, "slab", "grp", None),
            P("slab", "grp", None),
            P("slab", "grp", None),
            P("slab", "grp", None),
        ),
        out_specs=(P(None, "slab", "grp", None), P(None, "grp", "slab", None)),
        check_vma=False,
    )
```

profile of v0, /device:TPU:1, one launch (start us, length us, event | category | flops | bytes accessed | tf_op | source)
XLA Modules:
  0.0 816.2 jit_solution(5298064619461524530)
XLA Ops:
  3.5 5.4 collective-permute-start.2
  8.9 4.7 collective-permute-start
  13.6 1.9 collective-permute-start.1
  15.5 3.6 collective-permute-start.3
  21.9 4.0 collective-permute-start.7
  27.5 3.4 collective-permute-done.5
  31.6 3.8 collective-permute-start.9
  35.4 1.9 collective-permute-start.8
  37.3 3.1 collective-permute-done.8
  40.4 3.1 collective-permute-start.11
  44.8 3.4 collective-permute-done.10
  49.5 106.3 %all-reduce.9 = (f32[]{:T(128)}, f32[]{:T(128)}) all-reduce(f32[]{:T(128)} %get-tuple-element.11, f32[]{:T(128)} %get-tuple-element.10), channel_id=1, replica_groups=mesh['slab'=128,'grp'=4] {'slab','grp'}, use_global_device_ids=true, to_apply=%region_1.2 | all-reduce | flops 2 | bytes 16 | tf_op jit(solution)/shard_map/psum | solution.py:89
  157.7 95.6 %psum.58 = f32[]{:T(128)} all-reduce(f32[]{:T(128)} %multiply_reduce_fusion.3), channel_id=1, replica_groups=mesh['slab'=128,'grp'=4] {'slab','grp'}, use_global_device_ids=true, to_apply=%region_5.6 | all-reduce | flops 1 | bytes 8 | tf_op jit(solution)/shard_map/psum | solution.py:89
  254.8 2.2 collective-permute-start.13
  257.0 2.1 collective-permute-start.12
  259.1 2.9 collective-permute-done.12
  262.0 2.8 collective-permute-start.15
  266.1 3.4 collective-permute-done.14
  270.7 100.4 %psum.59 = f32[]{:T(128)} all-reduce(f32[]{:T(128)} %fusion.75), channel_id=1, replica_groups=mesh['slab'=128,'grp'=4] {'slab','grp'}, use_global_device_ids=true, to_apply=%region_7.8 | all-reduce | flops 1 | bytes 8 | tf_op jit(solution)/shard_map/psum | solution.py:89
  372.6 1.9 collective-permute-start.17
  374.5 2.4 collective-permute-start.16
  376.9 2.6 collective-permute-done.16
  379.6 3.7 collective-permute-start.19
  384.6 3.4 collective-permute-done.18
  388.6 3.6 collective-permute-start.21
  392.2 1.9 collective-permute-start.20
  394.2 3.1 collective-permute-done.20
  400.0 3.4 collective-permute-done.22
  404.7 105.3 %all-reduce.8 = (f32[]{:T(128)}, f32[]{:T(128)}) all-reduce(f32[]{:T(128)} %get-tuple-element.9, f32[]{:T(128)} %get-tuple-element.8), channel_id=1, replica_groups=mesh['slab'=128,'grp'=4] {'slab','grp'}, use_global_device_ids=true, to_apply=%region_9.10 | all-reduce | flops 2 | bytes 16 | tf_op jit(solution)/shard_map/psum | solution.py:89
  511.9 95.4 %psum.62 = f32[]{:T(128)} all-reduce(f32[]{:T(128)} %multiply_reduce_fusion), channel_id=1, replica_groups=mesh['slab'=128,'grp'=4] {'slab','grp'}, use_global_device_ids=true, to_apply=%region_13.14 | all-reduce | flops 1 | bytes 8 | tf_op jit(solution)/shard_map/psum | solution.py:89
  608.7 2.2 collective-permute-start.25
  611.0 2.1 collective-permute-start.24
  613.1 2.9 collective-permute-done.24
  616.0 3.4 collective-permute-start.27
  620.7 3.4 collective-permute-done.26
  625.4 100.4 %psum.63 = f32[]{:T(128)} all-reduce(f32[]{:T(128)} %fusion.15), channel_id=1, replica_groups=mesh['slab'=128,'grp'=4] {'slab','grp'}, use_global_device_ids=true, to_apply=%region_15.16 | all-reduce | flops 1 | bytes 8 | tf_op jit(solution)/shard_map/psum | solution.py:89
  729.2 2.4 collective-permute-start.28
  731.6 2.6 collective-permute-done.28
  734.2 3.7 collective-permute-start.31
  745.3 2.1 copy.79
  749.3 14.6 %all-to-all-start = ((f32[128,1,768]{2,1,0:T(1,128)}), f32[128,1,768]{2,1,0:T(1,128)S(1)}, u32[]{:S(2)}, u32[]{:S(2)}) async-start(f32[128,1,768]{2,1,0:T(1,128)} %reshape.66), calls=%async_computation | async-start | bytes 786432 | tf_op jit(solution)/shard_map/all_to_all | solution.py:144
  764.7 16.0 %all-to-all-done = f32[128,1,768]{2,1,0:T(1,128)S(1)} async-done(((f32[128,1,768]{2,1,0:T(1,128)}), f32[128,1,768]{2,1,0:T(1,128)S(1)}, u32[]{:S(2)}, u32[]{:S(2)}) %all-to-all-start) | async-done | bytes 393248 | tf_op jit(solution)/shard_map/all_to_all | solution.py:144
  783.8 2.6 copy.80
  786.4 3.8 all_to_all.10
  790.1 6.7 slice.508
  796.8 6.9 slice.509
  804.1 3.3 slice.514
  807.4 3.3 slice.515
  (126 shorter events, 43.5 us)
Async XLA Ops:
  0.6 2.8 copy-start.3
  0.6 12.9 %copy-start = (f32[3,16,8,128]{3,2,1,0:T(8,128)S(1)}, f32[3,16,8,128]{3,2,1,0:T(8,128)}, u32[]{:S(2)}) copy-start(f32[3,16,8,128]{3,2,1,0:T(8,128)} %param.27) | copy-start | bytes 589828
  1.7 29.5 %copy-start.1 = (f32[3,16,8,128]{3,2,1,0:T(8,128)S(1)}, f32[3,16,8,128]{3,2,1,0:T(8,128)}, u32[]{:S(2)}) copy-start(f32[3,16,8,128]{3,2,1,0:T(8,128)} %param.29) | copy-start | bytes 589828
  1.7 29.5 %copy-start.2 = (f32[3,16,8,128]{3,2,1,0:T(8,128)S(1)}, f32[3,16,8,128]{3,2,1,0:T(8,128)}, u32[]{:S(2)}) copy-start(f32[3,16,8,128]{3,2,1,0:T(8,128)} %param.28) | copy-start | bytes 589828
  1.7 29.5 %copy-start.5 = (f32[3]{0:T(128)S(1)}, f32[3]{0:T(128)}, u32[]{:S(2)}) copy-start(f32[3]{0:T(128)} %constant.9.clone) | copy-start | bytes 40
  1.7 29.5 %copy-start.6 = (f32[3]{0:T(128)S(1)}, f32[3]{0:T(128)}, u32[]{:S(2)}) copy-start(f32[3]{0:T(128)} %constant.8.clone) | copy-start | bytes 40
  1.8 29.5 %copy-start.7 = (f32[3]{0:T(128)S(1)}, f32[3]{0:T(128)}, u32[]{:S(2)}) copy-start(f32[3]{0:T(128)} %constant.7.clone) | copy-start | bytes 40
  3.5 15.7 %collective-permute-start.2 = (f32[1,8,128]{2,0,1:T(1,128)S(1)}, f32[1,8,128]{2,0,1:T(1,128)S(1)}, u32[]{:S(2)}, u32[]{:S(2)}) collective-permute-start(f32[1,8,128]{2,0,1:T(1,128)S(1)} %get-tuple-element.59), channel_id=1, source_target_pairs={{0,4},{4,8},{8,12},{12,16},{16,20},{20,24},{24,28},{28,32},{32,36}... | collective-permute-start | bytes 12296 | tf_op jit(solution)/shard_map/ppermute | solution.py:21
  8.9 10.4 %collective-permute-start = (f32[1,8,128]{2,0,1:T(1,128)S(1)}, f32[1,8,128]{2,0,1:T(1,128)S(1)}, u32[]{:S(2)}, u32[]{:S(2)}) collective-permute-start(f32[1,8,128]{2,0,1:T(1,128)S(1)} %get-tuple-element.60), channel_id=1, source_target_pairs={{4,0},{8,4},{12,8},{16,12},{20,16},{24,20},{28,24},{32,28},{36,32}... | collective-permute-start | bytes 12296 | tf_op jit(solution)/shard_map/ppermute | solution.py:24
  13.6 8.3 %collective-permute-start.1 = (f32[3,1,8,128]{3,1,2,0:T(1,128)S(1)}, f32[3,1,8,128]{3,1,2,0:T(1,128)S(1)}, u32[]{:S(2)}, u32[]{:S(2)}) collective-permute-start(f32[3,1,8,128]{3,1,2,0:T(1,128)S(1)} %bitcast.62), channel_id=1, source_target_pairs={{4,0},{8,4},{12,8},{16,12},{20,16},{24,20},{28,24},{32,28},{36,32}... | collective-permute-start | bytes 36872 | tf_op jit(solution)/shard_map/ppermute | solution.py:24
  15.5 6.3 collective-permute-start.3
  19.2 7.9 collective-permute-start.6
  20.5 6.7 collective-permute-start.4
  21.9 5.6 collective-permute-start.7
  25.9 5.0 collective-permute-start.5
  31.6 5.7 collective-permute-start.9
  35.4 5.0 collective-permute-start.8
  40.4 4.4 collective-permute-start.11
  43.5 4.7 collective-permute-start.10
  254.8 4.3 collective-permute-start.13
  257.0 5.0 collective-permute-start.12
  262.0 4.1 collective-permute-start.15
  264.8 4.7 collective-permute-start.14
  372.6 4.3 collective-permute-start.17
  374.5 5.0 collective-permute-start.16
  379.6 5.0 collective-permute-start.19
  383.2 4.7 collective-permute-start.18
  388.6 5.5 collective-permute-start.21
  392.2 5.0 collective-permute-start.20
  397.3 2.7 collective-permute-start.23
  398.7 4.7 collective-permute-start.22
  403.8 335.4 %copy-start.10 = (s32[4,2,32]{2,1,0:T(2,128)S(1)}, s32[4,2,32]{2,1,0:T(2,128)}, u32[]{:S(2)}) copy-start(s32[4,2,32]{2,1,0:T(2,128)} %param.32) | copy-start | bytes 3076
  608.7 4.3 collective-permute-start.25
  611.0 5.0 collective-permute-start.24
  616.0 4.7 collective-permute-start.27
  619.4 4.7 collective-permute-start.26
  727.2 4.4 collective-permute-start.29
  729.2 13.9 %copy-start.8 = (f32[16,16,1,1]{1,0,3,2:T(8,128)S(1)}, f32[16,16,1,1]{1,0,3,2:T(8,128)}, u32[]{:S(2)}) copy-start(f32[16,16,1,1]{1,0,3,2:T(8,128)} %constant.59) | copy-start | bytes 3076
  729.2 5.0 collective-permute-start.28
  734.2 7.0 collective-permute-start.31
  737.9 4.7 collective-permute-start.30
  739.2 4.3 copy-start.9
  739.5 4.6 copy-start.4
  749.3 31.3 %all-to-all-start = ((f32[128,1,768]{2,1,0:T(1,128)}), f32[128,1,768]{2,1,0:T(1,128)S(1)}, u32[]{:S(2)}, u32[]{:S(2)}) async-start(f32[128,1,768]{2,1,0:T(1,128)} %reshape.66), calls=%async_computation | async-start | bytes 786432 | tf_op jit(solution)/shard_map/all_to_all | solution.py:144
where the time goes:
time: 826 us; the launch traced here: 816 us
  blocking collectives  603 us (73%)
  starting transfers between devices  92.5 us (11%)
  waiting for transfers between devices  54.8 us (7%)
  local copies, waits for them, and re-layouts  41.9 us (5%)
  other arithmetic  11.5 us (1%)
  between operations  9.84 us (1%)
    psum x6, blocking collectives, single_sum(): return lax.psum(value, ('slab', 'grp'))  603 us
    ppermute x16, starting transfers between devices, with_halo(): lax.ppermute(lax.slice_in_dim(block, block.shape[dim] - width, None, axis...  48 us
    ppermute x16, waiting for transfers between devices, with_halo(): lax.ppermute(lax.slice_in_dim(block, 0, width, axis=dim), axis, backward)  38.8 us
    ppermute x16, starting transfers between devices, with_halo(): lax.ppermute(lax.slice_in_dim(block, 0, width, axis=dim), axis, backward)  29.8 us
  transfers between devices with their start and end apart: 33, of which 14 were waited for; matrix products, arithmetic and copies ran while one was open for 0% of the time, Pallas kernels for 0%

commit v1 on v0

--- a/solution.py
+++ b/solution.py
@@ -86,7 +86,7 @@
 
 
 def single_sum(value):
-    return lax.psum(value, ("slab", "grp"))
+    return lax.psum(lax.psum(value, "slab"), "grp")
 
 
 def lift(signal):

time: 826 us -> 1800 us (2.18)
  blocking collectives: 603 us -> 1540 us
  starting transfers between devices: 92.5 us -> 138 us
    psum x6 -> x12, blocking collectives: 603 us -> 1540 us  [single_sum(): return lax.psum(lax.psum(value, 'slab'), 'grp')]
    all_to_all x1, starting transfers between devices: 14.6 us -> 55.6 us  [body(): lax.all_to_all(moved, 'slab', split_axis=2, concat_axis=3, tiled=True)]
where the time goes in v1:
time: 1800 us; the launch traced here: 1790 us
  blocking collectives  1540 us (86%)
  starting transfers between devices  138 us (8%)
  waiting for transfers between devices  48.3 us (3%)
  local copies, waits for them, and re-layouts  41.9 us (2%)
    psum x12, blocking collectives, single_sum(): return lax.psum(lax.psum(value, 'slab'), 'grp')  1540 us
    all_to_all x1, starting transfers between devices, body(): lax.all_to_all(moved, 'slab', split_axis=2, concat_axis=3, tiled=True)  55.6 us
    ppermute x16, starting transfers between devices, with_halo(): lax.ppermute(lax.slice_in_dim(block, block.shape[dim] - width, None, axis...  46.6 us
    ppermute x16, starting transfers between devices, with_halo(): lax.ppermute(lax.slice_in_dim(block, 0, width, axis=dim), axis, backward)  36.3 us
  transfers between devices with their start and end apart: 33, of which 14 were waited for; matrix products, arithmetic and copies ran while one was open for 0% of the time, Pallas kernels for 0%

profile of v1, /device:TPU:1, one launch (start us, length us, event | category | flops | bytes accessed | tf_op | source)
XLA Modules:
  0.0 1791.7 jit_solution(1191226999319184656)
XLA Ops:
  3.5 5.4 collective-permute-start.2
  8.9 4.7 collective-permute-start
  13.6 1.9 collective-permute-start.1
  15.5 3.6 collective-permute-start.3
  21.9 4.0 collective-permute-start.7
  27.5 3.4 collective-permute-done.5
  31.6 3.8 collective-permute-start.9
  35.4 1.9 collective-permute-start.8
  37.3 3.1 collective-permute-done.8
  40.4 3.1 collective-permute-start.11
  44.8 3.4 collective-permute-done.10
  49.5 252.7 %all-reduce.9 = (f32[]{:T(128)}, f32[]{:T(128)}) all-reduce(f32[]{:T(128)} %get-tuple-element.11, f32[]{:T(128)} %get-tuple-element.10), channel_id=1, replica_groups=mesh['slab'=128,'grp'=4] {'slab'}, use_global_device_ids=true, to_apply=%region_1.2 | all-reduce | flops 2 | bytes 16 | tf_op jit(solution)/shard_map/psum | solution.py:89
  302.2 7.5 all-reduce.11
  311.7 251.0 %psum.116 = f32[]{:T(128)} all-reduce(f32[]{:T(128)} %multiply_reduce_fusion.3), channel_id=1, replica_groups=mesh['slab'=128,'grp'=4] {'slab'}, use_global_device_ids=true, to_apply=%region_7.8 | all-reduce | flops 1 | bytes 8 | tf_op jit(solution)/shard_map/psum | solution.py:89
  562.7 7.0 psum.117
  573.0 3.9 collective-permute-start.12
  578.0 3.0 collective-permute-start.15
  582.3 3.4 collective-permute-done.14
  587.0 248.3 %psum.118 = f32[]{:T(128)} all-reduce(f32[]{:T(128)} %fusion.75), channel_id=1, replica_groups=mesh['slab'=128,'grp'=4] {'slab'}, use_global_device_ids=true, to_apply=%region_10.11 | all-reduce | flops 1 | bytes 8 | tf_op jit(solution)/shard_map/psum | solution.py:89
  835.3 6.6 psum.119
  843.3 1.9 collective-permute-start.17
  845.2 3.7 collective-permute-start.16
  850.3 3.4 collective-permute-start.19
  854.9 3.4 collective-permute-done.18
  859.0 3.4 collective-permute-start.21
  864.3 3.1 collective-permute-done.20
  870.4 3.4 collective-permute-done.22
  875.0 246.3 %all-reduce.8 = (f32[]{:T(128)}, f32[]{:T(128)}) all-reduce(f32[]{:T(128)} %get-tuple-element.9, f32[]{:T(128)} %get-tuple-element.8), channel_id=1, replica_groups=mesh['slab'=128,'grp'=4] {'slab'}, use_global_device_ids=true, to_apply=%region_13.14 | all-reduce | flops 2 | bytes 16 | tf_op jit(solution)/shard_map/psum | solution.py:89
  1121.3 8.0 all-reduce.10
  1131.3 250.2 %psum.124 = f32[]{:T(128)} all-reduce(f32[]{:T(128)} %multiply_reduce_fusion), channel_id=1, replica_groups=mesh['slab'=128,'grp'=4] {'slab'}, use_global_device_ids=true, to_apply=%region_19.20 | all-reduce | flops 1 | bytes 8 | tf_op jit(solution)/shard_map/psum | solution.py:89
  1381.5 7.0 psum.125
  1391.8 3.9 collective-permute-start.24
  1396.9 3.0 collective-permute-start.27
  1401.2 3.4 collective-permute-done.26
  1405.8 248.3 %psum.126 = f32[]{:T(128)} all-reduce(f32[]{:T(128)} %fusion.15), channel_id=1, replica_groups=mesh['slab'=128,'grp'=4] {'slab'}, use_global_device_ids=true, to_apply=%region_22.23 | all-reduce | flops 1 | bytes 8 | tf_op jit(solution)/shard_map/psum | solution.py:89
  1654.1 6.6 psum.127
  1662.1 1.9 collective-permute-start.29
  1664.0 3.7 collective-permute-start.28
  1669.1 3.4 collective-permute-start.31
  1679.9 2.1 copy.79
  1683.8 55.6 %all-to-all-start = ((f32[128,1,768]{2,1,0:T(1,128)}), f32[128,1,768]{2,1,0:T(1,128)S(1)}, u32[]{:S(2)}, u32[]{:S(2)}) async-start(f32[128,1,768]{2,1,0:T(1,128)} %reshape.66), calls=%async_computation | async-start | bytes 786432 | tf_op jit(solution)/shard_map/all_to_all | solution.py:144
  1740.2 16.0 all-to-all-done
  1759.3 2.6 copy.80
  1761.9 3.8 all_to_all.10
  1765.7 6.7 slice.508
  1772.3 6.9 slice.509
  1779.6 3.3 slice.514
  1782.9 3.3 slice.515
  (132 shorter events, 52.4 us)
Async XLA Ops:
  0.6 2.8 copy-start.3
  0.6 12.9 copy-start
  1.7 29.5 %copy-start.1 = (f32[3,16,8,128]{3,2,1,0:T(8,128)S(1)}, f32[3,16,8,128]{3,2,1,0:T(8,128)}, u32[]{:S(2)}) copy-start(f32[3,16,8,128]{3,2,1,0:T(8,128)} %param.29) | copy-start | bytes 589828
  1.7 29.5 %copy-start.2 = (f32[3,16,8,128]{3,2,1,0:T(8,128)S(1)}, f32[3,16,8,128]{3,2,1,0:T(8,128)}, u32[]{:S(2)}) copy-start(f32[3,16,8,128]{3,2,1,0:T(8,128)} %param.28) | copy-start | bytes 589828
  1.7 29.5 %copy-start.5 = (f32[3]{0:T(128)S(1)}, f32[3]{0:T(128)}, u32[]{:S(2)}) copy-start(f32[3]{0:T(128)} %constant.9.clone) | copy-start | bytes 40
  1.7 29.5 %copy-start.6 = (f32[3]{0:T(128)S(1)}, f32[3]{0:T(128)}, u32[]{:S(2)}) copy-start(f32[3]{0:T(128)} %constant.8.clone) | copy-start | bytes 40
  1.8 29.5 %copy-start.7 = (f32[3]{0:T(128)S(1)}, f32[3]{0:T(128)}, u32[]{:S(2)}) copy-start(f32[3]{0:T(128)} %constant.7.clone) | copy-start | bytes 40
  3.5 15.7 collective-permute-start.2
  8.9 10.4 collective-permute-start
  13.6 8.3 collective-permute-start.1
  15.5 6.3 collective-permute-start.3
  19.2 7.9 collective-permute-start.6
  20.5 6.7 collective-permute-start.4
  21.9 5.6 collective-permute-start.7
  25.9 5.0 collective-permute-start.5
  31.6 5.7 collective-permute-start.9
  35.4 5.0 collective-permute-start.8
  40.4 4.4 collective-permute-start.11
  43.5 4.7 collective-permute-start.10
  571.1 5.8 collective-permute-start.13
  573.0 5.0 collective-permute-start.12
  578.0 4.3 collective-permute-start.15
  581.0 4.7 collective-permute-start.14
  843.3 5.6 collective-permute-start.17
  845.2 5.0 collective-permute-start.16
  850.3 4.7 collective-permute-start.19
  853.6 4.7 collective-permute-start.18
  859.0 5.3 collective-permute-start.21
  862.4 5.0 collective-permute-start.20
  867.4 3.0 collective-permute-start.23
  869.1 4.7 collective-permute-start.22
  874.1 800.1 %copy-start.10 = (s32[4,2,32]{2,1,0:T(2,128)S(1)}, s32[4,2,32]{2,1,0:T(2,128)}, u32[]{:S(2)}) copy-start(s32[4,2,32]{2,1,0:T(2,128)} %param.32) | copy-start | bytes 3076
  1389.9 5.8 collective-permute-start.25
  1391.8 5.0 collective-permute-start.24
  1396.9 4.3 collective-permute-start.27
  1399.8 4.7 collective-permute-start.26
  1662.1 5.6 collective-permute-start.29
  1664.0 13.6 copy-start.8
  1664.0 5.0 collective-permute-start.28
  1669.1 7.2 collective-permute-start.31
  1672.4 4.7 collective-permute-start.30
  1674.2 3.9 copy-start.9
  1674.6 4.1 copy-start.4
  1683.8 72.3 %all-to-all-start = ((f32[128,1,768]{2,1,0:T(1,128)}), f32[128,1,768]{2,1,0:T(1,128)S(1)}, u32[]{:S(2)}, u32[]{:S(2)}) async-start(f32[128,1,768]{2,1,0:T(1,128)} %reshape.66), calls=%async_computation | async-start | bytes 786432 | tf_op jit(solution)/shard_map/all_to_all | solution.py:144
